TPU v7x, 512 devices: a whole 4x8x8 slice. The times are simulated.
512 devices in a mesh: wave: 128 (over y, z, core), lev: 4 (over x).
Axes of the slice: x: 4, y: 8, z: 8, core: 2. Of those that a mesh axis runs over, the one named last changes fastest.
Arguments:
- spectral: bfloat16 [1280, 12, 2, 1280], P('wave', 'lev'), may hold values from -6 to 6
- legendre: bfloat16 [1280, 128, 1280], P('wave'), may hold values from -0.0048828125 to 0.0048828125
- wave_order: int32 [1280], replicated, may hold values from 0 to 1279, each once
- nlon: int32 [128], replicated, may hold values from 20 to 5136, as said below
Outputs:
- grid: float32 [12, 256, 5136], P(None, 'wave', 'lev')
Inputs may be any that keep to these rules, and one draw needn't show every extreme that they name: `wave_order`: each wavenumber 0 to 1279 stands at exactly one position. `nlon`: ascending and distinct, each 20 + 4 r for a whole r of 0 to 1279; the last is 5136.
All inputs are finite; a program needn't handle non-finite values.
Results may differ from a plain program's by a relative error of at most 0.0037.
Values may be sent and summed in bfloat16 or wider, within the bound.
A program may use at most 192 MiB of HBM per device.

v0:
```python
import math

import jax
import jax.numpy as jnp
from jax import lax
from jax.sharding import PartitionSpec as P


def fourier_table(wave_order, count, first, width):
    columns = first + jnp.arange(width, dtype=jnp.int32)
    phase = wave_order[:, None] * columns[None, :] % count
    angle = phase.astype(jnp.float32) * (2.0 * math.pi) / count.astype(jnp.float32)
    keep = (2 * wave_order[:, None] < count) & (columns[None, :] < count)
    weight = jnp.where(wave_order == 0, 1.0, 2.0).astype(jnp.float32)[:, None]
    cosine = jnp.where(keep, weight * jnp.cos(angle), 0.0).astype(jnp.bfloat16)
    sine = jnp.where(keep, -weight * jnp.sin(angle), 0.0).astype(jnp.bfloat16)
    return jnp.concatenate([cosine, sine], 0)


def synthesize(coeffs, wave_order, count, first, width):
    mixed = jnp.concatenate([coeffs[:, :, 0], coeffs[:, :, 1]], 0)
    table = fourier_table(wave_order, count, first, width)
    return lax.dot_general(
        mixed, table, (((0,), (0,)), ((), ())), preferred_element_type=jnp.float32
    )


def legendre_dense(spectral, legendre, local_waves):
    slots, fields, _, width = spectral.shape
    half = legendre.shape[1]
    offsets = jnp.arange(width, dtype=jnp.int32)
    live = offsets[None, :] < width - local_waves[:, None]
    coeffs = jnp.where(live[:, None, None, :], spectral, jnp.zeros((), jnp.bfloat16))
    coeffs = coeffs.reshape(slots, fields * 2, width // 2, 2)
    tables = legendre.reshape(slots, half, width // 2, 2)
    even = jnp.einsum(
        "phk,pck->phc", tables[..., 0], coeffs[..., 0], preferred_element_type=jnp.float32
    )
    odd = jnp.einsum(
        "phk,pck->phc", tables[..., 1], coeffs[..., 1], preferred_element_type=jnp.float32
    )
    return (even, odd)


def shards(spectral, legendre, wave_order, nlon):
    slots = legendre.shape[0]
    half = legendre.shape[1]
    width = legendre.shape[2]
    fields = spectral.shape[1]
    wave_id = lax.axis_index("wave")
    local_waves = lax.dynamic_slice_in_dim(wave_order, wave_id * slots, slots)
    even, odd = legendre_dense(spectral, legendre, local_waves)
    north = (even + odd).astype(jnp.bfloat16)
    south = (even - odd).astype(jnp.bfloat16)
    paired = jnp.stack([north, south[:, ::-1]], 2).reshape(slots, 2 * half, fields, 2)
    counts = (nlon[wave_id], nlon[half - 1 - wave_id])
    columns = 4 * width + 16
    quarter = columns // lax.axis_size("lev")
    gathered = lax.all_to_all(paired, "wave", split_axis=1, concat_axis=0, tiled=True)
    gathered = lax.all_gather(gathered, "lev", axis=2, tiled=True)
    first = lax.axis_index("lev") * quarter
    rows_out = [
        synthesize(gathered[:, lat], wave_order, counts[lat], first, quarter) for lat in range(2)
    ]
    return jnp.stack(rows_out, 1)


def solution(mesh):
    placed = (P("wave", "lev", None, None), P("wave", None, None), P(), P())
    return jax.shard_map(
        shards, mesh=mesh, in_specs=placed, out_specs=P(None, "wave", "lev"), check_vma=False
    )
```

profile of v0, /device:TPU:1, one launch (start us, length us, event | category | flops | bytes accessed | tf_op | source)
XLA Modules:
  0.0 285.3 jit_solution(7566103433650440720)
XLA Ops:
  0.0 0.8 dynamic-slice_subtract_fusion
  0.8 0.1 iota_compare_fusion
  0.9 1.1 broadcast_select_fusion
  1.9 1.0 copy.26
  3.0 4.1 %fusion.52 = (bf16[10,6,640,1]{0,3,2,1:T(2,128)(2,1)}, bf16[10,6,640,1]{0,3,2,1:T(2,128)(2,1)}) fusion(bf16[10,6,640,2]{0,3,2,1:T(2,128)(2,1)S(1)} %bitcast.57), kind=kLoop, calls=%fused_computation.74 | loop fusion | bytes 307200 | tf_op jit(solution)/shard_map/slice | solution.py:40
  7.1 3.7 %copy.42 = bf16[10,6,640,1]{2,1,0,3:T(8,128)(2,1)S(1)} copy(bf16[10,6,640,1]{0,3,2,1:T(2,128)(2,1)} %get-tuple-element.7) | data formatting | bytes 153600
  10.8 3.7 %copy.40 = bf16[10,6,640,1]{2,1,0,3:T(8,128)(2,1)S(1)} copy(bf16[10,6,640,1]{0,3,2,1:T(2,128)(2,1)} %get-tuple-element.8) | data formatting | bytes 153600
  14.4 4.3 %copy.28 = bf16[10,128,1280]{1,2,0:T(8,128)(2,1)S(1)} copy(bf16[10,128,1280]{2,1,0:T(8,128)(2,1)} %param.5) | data formatting | bytes 6553600 | tf_op args[1]
  18.7 6.2 %fusion.51 = (bf16[10,128,640,1]{1,3,2,0:T(2,128)(2,1)}, bf16[10,128,640,1]{1,3,2,0:T(2,128)(2,1)}) fusion(bf16[10,128,640,2]{1,3,2,0:T(2,128)(2,1)S(1)} %bitcast.56), kind=kLoop, calls=%fused_computation.73 | loop fusion | bytes 6553600 | tf_op jit(solution)/shard_map/slice | solution.py:40
  24.9 7.5 %copy.43 = bf16[10,128,640,1]{2,1,0,3:T(8,128)(2,1)} copy(bf16[10,128,640,1]{1,3,2,0:T(2,128)(2,1)} %get-tuple-element.5) | data formatting | bytes 3276800
  32.4 4.5 %copy.41 = bf16[10,128,640,1]{2,1,0,3:T(8,128)(2,1)} copy(bf16[10,128,640,1]{1,3,2,0:T(2,128)(2,1)S(1)} %copy-done) | data formatting | bytes 3276800
  37.0 2.1 fusion.32
  39.0 2.1 fusion.44
  41.1 0.1 rev.3
  41.2 0.3 copy.32
  41.5 1.2 copy.33
  42.7 18.4 %all-to-all-start = ((bf16[10,256,3,2]{0,3,2,1:T(2,128)(2,1)}), bf16[10,256,3,2]{0,3,2,1:T(2,128)(2,1)S(1)}, u32[]{:S(2)}, u32[]{:S(2)}) async-start(bf16[10,256,3,2]{0,3,2,1:T(2,128)(2,1)} %copy.33), calls=%async_computation | async-start | bytes 786432 | tf_op jit(solution)/shard_map/all_to_all | solution.py:59
  61.1 0.0 copy-done.4
  61.1 0.6 fusion.55
  64.3 1.3 multiply_compare_fusion.1
  65.6 1.3 fusion.46
  68.2 199.4 %fusion.5 = (bf16[1280,1284]{1,0:T(8,128)(2,1)}, bf16[1280,1284]{1,0:T(8,128)(2,1)}, bf16[1280,1284]{1,0:T(8,128)(2,1)}, bf16[1280,1284]{1,0:T(8,128)(2,1)}) fusion(f32[1280]{0:T(1024)S(1)} %get-tuple-element.26, f32[]{:T(128)S(6)} %convert_element_type.41, pred[]{:T(512)S(6)} %lt.86, s32[]{:T(128)S(6)} %select_n.50, s32[1284]{0:T(1024)S(1)} %iota_add_fusion, ...), kind=kLoop, calls=%fused_computation.13 | loop fusion | flops 57523200 | bytes 13173802 | tf_op jit(solution)/shard_map/convert_element_type | solution.py:16
  267.6 0.0 all-to-all-done
  267.6 0.1 copy.49
  267.6 0.6 all_to_all.16
  268.2 9.7 %all_gather.3 = bf16[1280,2,12,2]{0,3,2,1:T(2,128)(2,1)S(1)} all-gather(bf16[1280,2,3,2]{0,3,2,1:T(2,128)(2,1)S(1)} %all_to_all.16), channel_id=1, replica_groups=mesh['wave'=128,'lev'=4] {'lev'}, dimensions={2}, use_global_device_ids=true | all-gather | bytes 153600 | tf_op jit(solution)/shard_map/all_gather | solution.py:60
  277.9 0.1 slice_bitcast_fusion.1
  278.0 0.2 fusion.53
  278.2 4.3 %fusion.29 = f32[12,1,1284]{2,0,1:T(8,128)S(1)} fusion(bf16[1280,1284]{1,0:T(8,128)(2,1)} %get-tuple-element.19, bf16[1280,1284]{1,0:T(8,128)(2,1)} %get-tuple-element.22, bf16[1280,12]{0,1:T(8,128)(2,1)S(1)} %bitcast.65, bf16[1280,12]{0,1:T(8,128)(2,1)S(1)} %bitcast.63), kind=kOutput, calls=%fused_computation.35 | convolution fusion | flops 92160000 | bytes 6697152 | tf_op jit(solution)/shard_map/dot_general | solution.py:23
  282.5 0.9 copy-done.2
  283.4 1.1 fusion.26
  284.5 0.7 copy.35
  (16 shorter events, 0.1 us)
Async XLA Ops:
  24.9 7.5 %copy-start = (bf16[10,128,640,1]{1,3,2,0:T(2,128)(2,1)S(1)}, bf16[10,128,640,1]{1,3,2,0:T(2,128)(2,1)}, u32[]{:S(2)}) copy-start(bf16[10,128,640,1]{1,3,2,0:T(2,128)(2,1)} %get-tuple-element.6) | copy-start | bytes 4915204
  37.0 24.1 %copy-start.4 = (s32[128]{0:T(128)S(1)}, s32[128]{0:T(128)}, u32[]{:S(2)}) copy-start(s32[128]{0:T(128)} %param.7) | copy-start | bytes 1540
  37.0 27.3 %copy-start.3 = (s32[1280]{0:T(1024)S(1)}, s32[1280]{0:T(1024)}, u32[]{:S(2)}) copy-start(s32[1280]{0:T(1024)} %param.6) | copy-start | bytes 15364
  42.7 224.9 %all-to-all-start = ((bf16[10,256,3,2]{0,3,2,1:T(2,128)(2,1)}), bf16[10,256,3,2]{0,3,2,1:T(2,128)(2,1)S(1)}, u32[]{:S(2)}, u32[]{:S(2)}) async-start(bf16[10,256,3,2]{0,3,2,1:T(2,128)(2,1)} %copy.33), calls=%async_computation | async-start | bytes 786432 | tf_op jit(solution)/shard_map/all_to_all | solution.py:59
  278.2 4.3 %copy-start.1 = (bf16[1280,1284]{1,0:T(8,128)(2,1)S(1)}, bf16[1280,1284]{1,0:T(8,128)(2,1)}, u32[]{:S(2)}) copy-start(bf16[1280,1284]{1,0:T(8,128)(2,1)} %get-tuple-element.20) | copy-start | bytes 9861124
  278.2 5.2 %copy-start.2 = (bf16[1280,1284]{1,0:T(8,128)(2,1)S(1)}, bf16[1280,1284]{1,0:T(8,128)(2,1)}, u32[]{:S(2)}) copy-start(bf16[1280,1284]{1,0:T(8,128)(2,1)} %get-tuple-element.21) | copy-start | bytes 9861124
where the time goes:
time: 288 us; the launch traced here: 285 us
  other arithmetic  204 us (71%)
  local copies, waits for them, and re-layouts  39.7 us (14%)
  starting transfers between devices  18.4 us (6%)
  blocking collectives  9.67 us (3%)
  matrix products  9.47 us (3%)
  between operations  4.07 us (1%)
    convert_element_type x1, other arithmetic, fourier_table(): sine = jnp.where(keep, -weight * jnp.sin(angle), 0.0).astype(jnp.bfloat16)  199 us
    unnamed x19, local copies, waits for them, and re-layouts  24.6 us
    all_to_all x1, starting transfers between devices, shards(): lax.all_to_all(paired, 'wave', split_axis=1, concat_axis=0, tiled=True)  18.4 us
    all_gather x1, blocking collectives, shards(): gathered = lax.all_gather(gathered, 'lev', axis=2, tiled=True)  9.67 us
    slice x1, local copies, waits for them, and re-layouts, legendre_dense(): tables[..., 1]  6.17 us
  transfers between devices with their start and end apart: 1, of which 0 were waited for; matrix products, arithmetic and copies ran while one was open for 71% of the time, Pallas kernels for 0%

commit v1 on v0

v1 whole, which is shorter than its diff:
```python
import functools
import math

import jax
import jax.numpy as jnp
from jax import lax
from jax.experimental import pallas as pl
from jax.experimental.pallas import tpu as pltpu
from jax.sharding import PartitionSpec as P

MESH = pl.DeviceIdType.MESH
F32 = jnp.float32
BF16 = jnp.bfloat16
LANES = 128
HALF = LANES // 2
SPAN = 256
STEP = 16
NT = (((1,), (1,)), ((), ()))


def iota(shape, dim):
    return lax.broadcasted_iota(jnp.int32, shape, dim)


def sincos(x, n, inv, far):
    if far:
        x = x - jnp.floor(x * inv + 0.5) * n
    x = 4.0 * x
    k = jnp.floor(x * inv + 0.5)
    a = (x - k * n) * (inv * (math.pi / 2))
    q = k.astype(jnp.int32)
    z = a * a
    s = a + a * z * (-1.6666654611e-1 + z * (8.3321608736e-3 + z * -1.9515295891e-4))
    c = 1.0 - 0.5 * z + z * z * (
        4.166664568298827e-2 + z * (-1.388731625493765e-3 + z * 2.443315711809948e-5)
    )
    odd = (q & 1) == 1
    cos, sin = jnp.where(odd, s, c), jnp.where(odd, c, s)
    cos = jnp.where(((q + 1) & 2) == 2, -cos, cos)
    sin = jnp.where((q & 2) == 2, -sin, sin)
    return cos, sin


def kernel(
    chips, cores, levs, quarter,
    spec_ref, leg_ref, order_s, nlon_s, order_v, out_ref,
    lbuf, xbuf, zbuf, send1, recv1, send2, recv2, table, twist, mixed, gbuf, vbuf,
    leg_sem, s1_sem, r1_sem, s2_sem, r2_sem,
):
    slots, half, width = leg_ref.shape
    fields = spec_ref.shape[1]
    total = fields * levs
    w = lax.axis_index("wave")
    x = lax.axis_index("lev")
    chip, core = w // cores, lax.rem(w, cores)

    def leg_copy(p):
        return pltpu.make_async_copy(leg_ref.at[p], lbuf.at[p], leg_sem.at[p])

    for p in range(slots):
        leg_copy(p).start()

    barrier = pltpu.get_barrier_semaphore()

    def near(d):
        return lax.rem(core + d // levs, cores), lax.rem(x + d % levs, levs)

    def greet(d, carry):
        there = lax.rem(chip + d, chips) * cores + core
        pl.semaphore_signal(barrier, inc=1, device_id=(there, x), device_id_type=MESH)
        return carry

    lax.fori_loop(1, chips, greet, 0)
    group = cores * levs
    for d in range(1, group):
        c2, x2 = near(d)
        pl.semaphore_signal(barrier, inc=1, device_id=(chip * cores + c2, x2), device_id_type=MESH)

    rows_v = order_v.shape[0]
    lane = iota((1, half), 1)
    device = lax.rem(lane, chips) * cores + lane // chips
    high, low = (order_v[...] // 256).astype(F32).astype(BF16), lax.rem(order_v[...], 256).astype(F32).astype(BF16)
    for p in range(slots):
        place = device * slots + p
        pick = (iota((order_v.shape[1], half), 0) == lax.rem(place, order_v.shape[1])).astype(F32).astype(BF16)
        both = 256.0 * jnp.dot(high, pick, preferred_element_type=F32) + jnp.dot(low, pick, preferred_element_type=F32)
        row = iota((rows_v, half), 0) == place // order_v.shape[1]
        vbuf[p : p + 1] = jnp.sum(jnp.where(row, both, 0.0), 0, keepdims=True)

    offset = iota((1, width), 1)
    parity = (1 - 2 * lax.rem(offset, 2)).astype(F32)
    zbuf[...] = jnp.zeros_like(zbuf)
    for p in range(slots):
        live = offset < width - order_s[w * slots + p]
        for f in range(fields):
            coeffs = jnp.where(live, spec_ref[p, f].astype(F32), 0.0)
            xbuf[p, 2 * f : 2 * f + 2] = coeffs
            xbuf[p, 8 + 2 * f : 8 + 2 * f + 2] = coeffs * parity
        leg_copy(p).wait()
        sums = lax.dot_general(xbuf[p].astype(BF16), lbuf[p], NT, preferred_element_type=F32)
        n = 2 * fields
        zbuf[n * p : n * p + n] = sums[0:n]
        zbuf[HALF + n * p : HALF + n * p + n] = sums[8 : 8 + n]

    z = zbuf[...].astype(BF16).astype(F32)
    north = iota((LANES, half), 0) < HALF
    pair = jnp.concatenate([jnp.where(north, z, 0.0), jnp.where(north, 0.0, z)], 1).astype(BF16)
    h, g = iota((half, 2 * half), 0), iota((half, 2 * half), 1)
    route = ((g == h) | ((g == 2 * half - 1 - h) & (g >= half))).astype(F32).astype(BF16)
    rows = lax.dot_general(route, pair, NT, preferred_element_type=F32)
    send1[...] = rows.reshape(chips, cores, LANES)

    pl.semaphore_wait(barrier, chips - 1 + group - 1)

    def first_copy(src, dst, there):
        return pltpu.make_async_remote_copy(
            src_ref=src, dst_ref=dst, send_sem=s1_sem, recv_sem=r1_sem,
            device_id=(there, x), device_id_type=MESH,
        )

    def push(d, carry):
        to = lax.rem(chip + d, chips)
        first_copy(send1.at[to], recv1.at[chip], to * cores + core).start()
        return carry

    lax.fori_loop(1, chips, push, 0)
    recv1[pl.ds(chip, 1)] = send1[pl.ds(chip, 1)]

    counts = [nlon_s[w].astype(F32), nlon_s[half - 1 - w].astype(F32)]
    inverse = [1.0 / jnp.full((1, half), n, F32) for n in counts]
    fine = iota((STEP, half), 0).astype(F32)
    for ns in range(2):
        n, inv = counts[ns], inverse[ns]
        for p in range(slots):
            m = vbuf[p : p + 1]
            cb, sb = sincos(m * fine, n, inv, False)
            ca, sa = sincos(m * (STEP * fine), n, inv, False)
            for a in range(SPAN // STEP):
                c1, s1 = ca[a : a + 1], sa[a : a + 1]
                here = pl.ds(a * STEP, STEP)
                table[ns, here, p * half : (p + 1) * half] = (c1 * cb - s1 * sb).astype(BF16)
                table[ns, here, (slots + p) * half : (slots + p + 1) * half] = (-(c1 * sb) - s1 * cb).astype(BF16)

    everything = first_copy(send1.at[pl.ds(0, chips - 1)], recv1.at[pl.ds(0, chips - 1)], lax.rem(chip + 1, chips) * cores + core)
    everything.wait_recv()
    got = recv1[...]
    for c in range(cores):
        send2[c] = got[:, c, :].astype(BF16)

    second = []
    for d in range(1, group):
        c2, x2 = near(d)
        second.append(
            pltpu.make_async_remote_copy(
                src_ref=send2.at[c2], dst_ref=recv2.at[x, core], send_sem=s2_sem.at[d], recv_sem=r2_sem.at[d],
                device_id=(chip * cores + c2, x2), device_id_type=MESH,
            )
        )
    for copy in second:
        copy.start()
    recv2[x, core] = send2[core]

    first = x * quarter
    spans = pl.cdiv(quarter, SPAN)
    starts = (first + SPAN * iota((8, half), 0)).astype(F32)
    for ns in range(2):
        n, inv = counts[ns], inverse[ns]
        for p in range(slots):
            m = vbuf[p : p + 1]
            weight = jnp.where(2.0 * m < n, jnp.where(m == 0.0, 1.0, 2.0), 0.0)
            ct, st = sincos(m * starts, n, inv, True)
            twist[ns, p, 0] = ct * weight
            twist[ns, p, 1] = st * weight

    f16 = iota((STEP, LANES), 0)
    gap = iota((STEP, LANES), 1) - 2 * f16
    parts = [(f16 >= fields * v) & (f16 < fields * (v + 1)) for v in range(levs)]
    picks = []
    for ns in range(2):
        for c in range(2):
            for p in range(slots):
                at = HALF * ns + 2 * fields * p + c
                picks.append(
                    jnp.concatenate(
                        [((gap == at - 2 * fields * v) & parts[v]).astype(F32) for v in range(levs)], 1
                    ).astype(BF16)
                )
    choice = jnp.concatenate(picks, 0)

    for copy in second:
        copy.wait_recv()
    arrived = jnp.concatenate([recv2[v].reshape(half, LANES) for v in range(levs)], 1)
    mixed[...] = lax.dot_general(choice, arrived, NT, preferred_element_type=F32)

    for ns in range(2):
        for p in range(slots):
            at = STEP * (2 * slots * ns + p)
            re, im = mixed[at : at + STEP], mixed[at + STEP * slots : at + STEP * slots + STEP]
            for s in range(spans):
                ct, st = twist[ns, p, 0, s : s + 1], twist[ns, p, 1, s : s + 1]
                here = pl.ds(s * STEP, STEP)
                gbuf[ns, here, p * half : (p + 1) * half] = (re * ct - im * st).astype(BF16)
                gbuf[ns, here, (slots + p) * half : (slots + p + 1) * half] = (re * st + im * ct).astype(BF16)
        grid = lax.dot_general(gbuf[ns], table[ns], NT, preferred_element_type=F32)
        for s in range(spans):
            size = min(SPAN, quarter - s * SPAN)
            column = first + s * SPAN + iota((total, size), 1)
            keep = column < nlon_s[w if ns == 0 else half - 1 - w]
            out_ref[ns, :, s * SPAN : s * SPAN + size] = jnp.where(
                keep, grid[s * STEP : s * STEP + total, :size], 0.0
            )
    everything.wait_send()
    for copy in second:
        copy.wait_send()


def shards(spectral, legendre, wave_order, nlon):
    slots, half, width = legendre.shape
    fields = spectral.shape[1]
    waves, levs = lax.axis_size("wave"), lax.axis_size("lev")
    cores = 2
    chips = waves // cores
    quarter = (4 * width + 16) // levs
    spans = pl.cdiv(quarter, SPAN)
    vmem = pl.BlockSpec(memory_space=pltpu.VMEM)
    smem = pl.BlockSpec(memory_space=pltpu.SMEM)
    dma = pltpu.SemaphoreType.DMA
    order_rows = wave_order.reshape(-1, min(LANES, wave_order.shape[0] // slots))
    grid = pl.pallas_call(
        functools.partial(kernel, chips, cores, levs, quarter),
        out_shape=jax.ShapeDtypeStruct((2, fields * levs, quarter), F32),
        in_specs=[vmem, pl.BlockSpec(memory_space=pl.ANY), smem, smem, vmem],
        out_specs=vmem,
        scratch_shapes=[
            pltpu.VMEM((slots, half, width), BF16),
            pltpu.VMEM((slots, 16, width), F32),
            pltpu.VMEM((LANES, half), F32),
            pltpu.VMEM((chips, cores, LANES), F32),
            pltpu.VMEM((chips, cores, LANES), F32),
            pltpu.VMEM((cores, chips, LANES), BF16),
            pltpu.VMEM((levs, cores, chips, LANES), BF16),
            pltpu.VMEM((2, SPAN, 2 * slots * half), BF16),
            pltpu.VMEM((2, slots, 2, 8, half), F32),
            pltpu.VMEM((4 * slots * STEP, half), F32),
            pltpu.VMEM((2, spans * STEP, 2 * slots * half), BF16),
            pltpu.VMEM((16, half), F32),
            dma((slots,)),
            dma,
            dma,
            dma((cores * levs,)),
            dma((cores * levs,)),
        ],
        compiler_params=pltpu.CompilerParams(
            collective_id=0, has_side_effects=True, vmem_limit_bytes=40 * 1024 * 1024
        ),
    )(spectral, legendre, wave_order, nlon, order_rows)
    return jnp.transpose(grid, (1, 0, 2))


def solution(mesh):
    placed = (P("wave", "lev", None, None), P("wave", None, None), P(), P())
    return jax.shard_map(
        shards, mesh=mesh, in_specs=placed, out_specs=P(None, "wave", "lev"), check_vma=False
    )
```

time: 288 us -> 36.1 us (0.13)
  other arithmetic: 204 us -> 0 us
  local copies, waits for them, and re-layouts: 39.7 us -> 4.92 us
  Pallas kernels: 0 us -> 30.9 us
  starting transfers between devices: 18.4 us -> 0 us
  blocking collectives: 9.67 us -> 0 us
  matrix products: 9.47 us -> 0 us
  between operations: 4.07 us -> 0.01 us
    convert_element_type x1 -> x0, other arithmetic: 199 us -> none  [fourier_table(): sine = jnp.where(keep, -weight * jnp.sin(angle), 0.0).astype(jnp.bfloat16)]
    pallas_call x0 -> x1, Pallas kernels: none -> 30.9 us  [shards(): pl.pallas_call(functools.partial(kernel, chips, cores, levs, quarter), ou...]
    unnamed x19 -> x8, local copies, waits for them, and re-layouts: 24.6 us -> 4.19 us
    all_to_all x1 -> x0, starting transfers between devices: 18.4 us -> none  [shards(): lax.all_to_all(paired, 'wave', split_axis=1, concat_axis=0, tiled=True)]
    slice x3 -> x0, local copies, waits for them, and re-layouts: 10.4 us -> none  [the longest x1 6.17 us: legendre_dense(): tables[..., 1]]
    all_gather x1 -> x0, blocking collectives: 9.67 us -> none  [shards(): gathered = lax.all_gather(gathered, 'lev', axis=2, tiled=True)]
    dot_general x4 -> x0, matrix products: 9.47 us -> none  [the longest x2 5.36 us: synthesize(): lax.dot_general(mixed, table, (((0,), (0,)), ((), ())), preferred_element...]
  transfers between devices with their start and end apart: 1 -> 0, of which waited for: 0 -> 0; matrix products, arithmetic and copies ran while one was open for 71% -> 0% of each run, Pallas kernels for 0% -> 0%
where the time goes in v1:
time: 36.1 us; the launch traced here: 35.8 us
  Pallas kernels  30.9 us (86%)
  local copies, waits for them, and re-layouts  4.92 us (14%)
    pallas_call x1, Pallas kernels, shards(): pl.pallas_call(functools.partial(kernel, chips, cores, levs, quarter), ou...  30.9 us
    unnamed x8, local copies, waits for them, and re-layouts  4.19 us
    transpose x1, local copies, waits for them, and re-layouts, shards(): return jnp.transpose(grid, (1, 0, 2))  0.73 us

profile of v1, /device:TPU:1, one launch (start us, length us, event | category | flops | bytes accessed | tf_op | source)
XLA Modules:
  0.0 35.8 jit_solution(4646670489322551515)
XLA Ops:
  0.0 0.0 copy-start
  0.0 1.9 %copy-done = bf16[10,128,1280]{2,1,0:T(8,128)(2,1)S(1)} copy-done((bf16[10,128,1280]{2,1,0:T(8,128)(2,1)S(1)}, bf16[10,128,1280]{2,1,0:T(8,128)(2,1)}, u32[]{:S(2)}) %copy-start) | copy-done | bytes 3276824
  1.9 0.0 copy-start.1
  1.9 0.9 %copy-done.1 = bf16[10,3,2,1280]{3,2,1,0:T(2,128)(2,1)S(1)} copy-done((bf16[10,3,2,1280]{3,2,1,0:T(2,128)(2,1)S(1)}, bf16[10,3,2,1280]{3,2,1,0:T(2,128)(2,1)}, u32[]{:S(2)}) %copy-start.1) | copy-done | bytes 153624
  2.8 0.0 copy-start.2
  2.8 0.7 %copy-done.2 = s32[1280]{0:T(1024)S(1)} copy-done((s32[1280]{0:T(1024)S(1)}, s32[1280]{0:T(1024)}, u32[]{:S(2)}) %copy-start.2) | copy-done | bytes 5144
  3.5 0.0 copy-start.3
  3.5 0.7 %copy-done.3 = s32[128]{0:T(128)S(1)} copy-done((s32[128]{0:T(128)S(1)}, s32[128]{0:T(128)}, u32[]{:S(2)}) %copy-start.3) | copy-done | bytes 536
  4.2 30.9 %shard_map.46 = f32[2,12,1284]{2,1,0:T(8,128)S(1)} custom-call(bf16[10,3,2,1280]{3,2,1,0:T(2,128)(2,1)S(1)} %copy-done.1, bf16[10,128,1280]{2,1,0:T(8,128)(2,1)S(1)} %copy-done, s32[1280]{0:T(1024)S(1)} %copy-done.2, s32[128]{0:T(128)S(1)} %copy-done.3, s32[10,128]{1,0:T(8,128)S(1)} %bitcast.3), custom_call_target="tpu_custom_call" | custom-call | tf_op jit(solution)/shard_map/pallas_call | solution.py:229
  35.1 0.7 %copy.5 = f32[12,2,1284]{2,1,0:T(2,128)} copy(f32[12,2,1284]{2,0,1:T(8,128)S(1)} %bitcast.2) | data formatting | bytes 246528 | tf_op jit(solution)/shard_map/transpose | solution.py:257
Async XLA Ops:
  0.0 1.9 %copy-start = (bf16[10,128,1280]{2,1,0:T(8,128)(2,1)S(1)}, bf16[10,128,1280]{2,1,0:T(8,128)(2,1)}, u32[]{:S(2)}) copy-start(bf16[10,128,1280]{2,1,0:T(8,128)(2,1)} %leg_ref.1) | copy-start | bytes 9830404
  1.9 0.9 %copy-start.1 = (bf16[10,3,2,1280]{3,2,1,0:T(2,128)(2,1)S(1)}, bf16[10,3,2,1280]{3,2,1,0:T(2,128)(2,1)}, u32[]{:S(2)}) copy-start(bf16[10,3,2,1280]{3,2,1,0:T(2,128)(2,1)} %spec_ref.1) | copy-start | bytes 460804
  2.8 0.7 %copy-start.2 = (s32[1280]{0:T(1024)S(1)}, s32[1280]{0:T(1024)}, u32[]{:S(2)}) copy-start(s32[1280]{0:T(1024)} %order_s.1) | copy-start | bytes 15364
  3.5 0.7 %copy-start.3 = (s32[128]{0:T(128)S(1)}, s32[128]{0:T(128)}, u32[]{:S(2)}) copy-start(s32[128]{0:T(128)} %nlon_s.1) | copy-start | bytes 1540

commit v2 on v1

v2 whole, which is shorter than its diff:
```python
import functools
import math

import jax
import jax.numpy as jnp
from jax import lax
from jax.experimental import pallas as pl
from jax.experimental.pallas import tpu as pltpu
from jax.sharding import PartitionSpec as P

MESH = pl.DeviceIdType.MESH
F32 = jnp.float32
BF16 = jnp.bfloat16
LANES = 128
HALF = LANES // 2
SPAN = 256
STEP = 16
NT = (((1,), (1,)), ((), ()))


def iota(shape, dim):
    return lax.broadcasted_iota(jnp.int32, shape, dim)


def sincos(x, n, inv, far):
    if far:
        x = x - jnp.floor(x * inv + 0.5) * n
    x = 4.0 * x
    k = jnp.floor(x * inv + 0.5)
    a = (x - k * n) * (inv * (math.pi / 2))
    q = k.astype(jnp.int32)
    z = a * a
    s = a + a * z * (-1.6666654611e-1 + z * (8.3321608736e-3 + z * -1.9515295891e-4))
    c = 1.0 - 0.5 * z + z * z * (
        4.166664568298827e-2 + z * (-1.388731625493765e-3 + z * 2.443315711809948e-5)
    )
    odd = (q & 1) == 1
    cos, sin = jnp.where(odd, s, c), jnp.where(odd, c, s)
    cos = jnp.where(((q + 1) & 2) == 2, -cos, cos)
    sin = jnp.where((q & 2) == 2, -sin, sin)
    return cos, sin


def kernel(
    chips, cores, levs, quarter,
    spec_hbm, leg_ref, order_hbm, nlon_hbm, rows_hbm, out_ref,
    spec_ref, order_s, nlon_s, order_v, lbuf, xbuf, zbuf, send1, recv1, send2, recv2, table, twist, mixed, gbuf, vbuf,
    in_sem, leg_sem, s1_sem, r1_sem, s2_sem, r2_sem,
):
    slots, half, width = leg_ref.shape
    fields = spec_ref.shape[1]
    total = fields * levs
    w = lax.axis_index("wave")
    x = lax.axis_index("lev")
    chip, core = w // cores, lax.rem(w, cores)

    inputs = [
        pltpu.make_async_copy(src, dst, in_sem.at[i])
        for i, (src, dst) in enumerate(
            [(spec_hbm, spec_ref), (order_hbm, order_s), (nlon_hbm, nlon_s), (rows_hbm, order_v)]
        )
    ]
    legs = [pltpu.make_async_copy(leg_ref.at[p], lbuf.at[p], leg_sem.at[p]) for p in range(slots)]

    side = math.isqrt(chips)
    y, z = chip // side, lax.rem(chip, side)
    ys = [lax.rem(y + d, side) for d in range(side)]
    zs = [lax.rem(z + d, side) for d in range(side)]
    cs = [lax.rem(core + d, cores) for d in range(cores)]
    xs = [lax.rem(x + d, levs) for d in range(levs)]

    def hops(d, n):
        return min(d, n - d)

    def far_first(n1, n2, weight):
        pairs = [(d, e) for d in range(n1) for e in range(n2) if d or e]
        return sorted(pairs, key=lambda d: -hops(d[0], n1) - weight * hops(d[1], n2))

    mates = [(ys[d], cs[e]) for d, e in far_first(side, cores, 0.1)]
    rest = [(zs[d], xs[e]) for d, e in far_first(side, levs, 1)]

    def mate_id(there):
        return ((there[0] * side + z) * cores + there[1], x)

    def rest_id(there):
        return ((y * side + there[0]) * cores + core, there[1])

    barrier = pltpu.get_barrier_semaphore()
    for i, there in enumerate([rest_id(r) for r in rest] + [mate_id(r) for r in mates]):
        if i == side:
            for copy in inputs + legs:
                copy.start()
        pl.semaphore_signal(barrier, inc=1, device_id=there, device_id_type=MESH)
    for copy in inputs:
        copy.wait()

    offset = iota((1, width), 1)
    parity = (1 - 2 * lax.rem(offset, 2)).astype(F32)
    zbuf[...] = jnp.zeros_like(zbuf)
    n = 2 * fields
    for p in range(slots):
        live = offset < width - order_s[w * slots + p]
        for f in range(fields):
            coeffs = jnp.where(live, spec_ref[p, f].astype(F32), 0.0)
            xbuf[p, 2 * f : 2 * f + 2] = coeffs
            xbuf[p, 8 + 2 * f : 8 + 2 * f + 2] = coeffs * parity
    for p in range(slots):
        legs[p].wait()
        sums = lax.dot_general(xbuf[p].astype(BF16), lbuf[p], NT, preferred_element_type=F32)
        zbuf[n * p : n * p + n] = sums[0:n]
        zbuf[HALF + n * p : HALF + n * p + n] = sums[8 : 8 + n]

    total_mates = side * cores
    values = zbuf[...].astype(BF16).astype(F32)
    north = iota((LANES, half), 0) < HALF
    pair = jnp.concatenate([jnp.where(north, values, 0.0), jnp.where(north, 0.0, values)], 1).astype(BF16)
    r, g = iota((half, 2 * half), 0), iota((half, 2 * half), 1)
    h = (r // total_mates * side + lax.rem(r, side)) * cores + lax.rem(r // side, cores)
    route = ((g == h) | ((g == 2 * half - 1 - h) & (g >= half))).astype(F32).astype(BF16)
    send1[...] = lax.dot_general(route, pair, NT, preferred_element_type=F32)

    pl.semaphore_wait(barrier, len(mates) + len(rest))

    def block(i):
        return pl.ds(pl.multiple_of(i * side, side), side)

    def remote(src, dst, sems, there):
        return pltpu.make_async_remote_copy(
            src_ref=src, dst_ref=dst, send_sem=sems[0], recv_sem=sems[1], device_id=there, device_id_type=MESH
        )

    own = y * cores + core
    for there in mates:
        remote(send1.at[block(there[0] * cores + there[1])], recv1.at[block(own)], (s1_sem, r1_sem), mate_id(there)).start()
    recv1[block(own)] = send1[block(own)]

    rows_v = order_v.shape[0]
    lane = iota((1, half), 1)
    device = (lax.rem(lane, total_mates) // cores * side + lane // total_mates) * cores + lax.rem(lane, cores)
    high, low = (order_v[...] // 256).astype(F32).astype(BF16), lax.rem(order_v[...], 256).astype(F32).astype(BF16)
    for p in range(slots):
        place = device * slots + p
        pick = (iota((order_v.shape[1], half), 0) == lax.rem(place, order_v.shape[1])).astype(F32).astype(BF16)
        both = 256.0 * jnp.dot(high, pick, preferred_element_type=F32) + jnp.dot(low, pick, preferred_element_type=F32)
        row = iota((rows_v, half), 0) == place // order_v.shape[1]
        vbuf[p : p + 1] = jnp.sum(jnp.where(row, both, 0.0), 0, keepdims=True)

    counts = [nlon_s[w].astype(F32), nlon_s[half - 1 - w].astype(F32)]
    inverse = [1.0 / jnp.full((1, half), n, F32) for n in counts]
    fine = iota((STEP, half), 0).astype(F32)
    for ns in range(2):
        n, inv = counts[ns], inverse[ns]
        for p in range(slots):
            m = vbuf[p : p + 1]
            cb, sb = sincos(m * fine, n, inv, False)
            ca, sa = sincos(m * (STEP * fine), n, inv, False)
            for a in range(SPAN // STEP):
                c1, s1 = ca[a : a + 1], sa[a : a + 1]
                here = pl.ds(a * STEP, STEP)
                table[ns, here, p * half : (p + 1) * half] = (c1 * cb - s1 * sb).astype(BF16)
                table[ns, here, (slots + p) * half : (slots + p + 1) * half] = (-(c1 * sb) - s1 * cb).astype(BF16)

    most = pl.ds(0, side * (total_mates - 1))
    first_all = remote(send1.at[most], recv1.at[most], (s1_sem, r1_sem), mate_id(mates[0]))
    first_all.wait_recv()
    for i in range(side):
        send2[i] = recv1[pl.ds(i, total_mates, stride=side)].astype(BF16)
    for there in rest:
        remote(send2.at[there[0]], recv2.at[x * side + z], (s2_sem, r2_sem), rest_id(there)).start()
    recv2[x * side + z] = send2[z]

    first = x * quarter
    spans = pl.cdiv(quarter, SPAN)
    starts = (first + SPAN * iota((8, half), 0)).astype(F32)
    for ns in range(2):
        n, inv = counts[ns], inverse[ns]
        for p in range(slots):
            m = vbuf[p : p + 1]
            weight = jnp.where(2.0 * m < n, jnp.where(m == 0.0, 1.0, 2.0), 0.0)
            ct, st = sincos(m * starts, n, inv, True)
            twist[ns, p, 0] = ct * weight
            twist[ns, p, 1] = st * weight

    f16 = iota((STEP, LANES), 0)
    gap = iota((STEP, LANES), 1) - 2 * f16
    parts = [(f16 >= fields * v) & (f16 < fields * (v + 1)) for v in range(levs)]
    picks = []
    for ns in range(2):
        for c in range(2):
            for p in range(slots):
                at = HALF * ns + 2 * fields * p + c
                picks.append(
                    jnp.concatenate(
                        [((gap == at - 2 * fields * v) & parts[v]).astype(F32) for v in range(levs)], 1
                    ).astype(BF16)
                )
    choice = jnp.concatenate(picks, 0)

    most = pl.ds(0, side * levs - 1)
    second_all = remote(recv2.at[most], recv2.at[most], (s2_sem, r2_sem), rest_id(rest[0]))
    second_all.wait_recv()
    arrived = jnp.concatenate(
        [recv2[v * side : (v + 1) * side].reshape(half, LANES) for v in range(levs)], 1
    )
    mixed[...] = lax.dot_general(choice, arrived, NT, preferred_element_type=F32)

    for ns in range(2):
        for p in range(slots):
            at = STEP * (2 * slots * ns + p)
            re, im = mixed[at : at + STEP], mixed[at + STEP * slots : at + STEP * slots + STEP]
            for s in range(spans):
                ct, st = twist[ns, p, 0, s : s + 1], twist[ns, p, 1, s : s + 1]
                here = pl.ds(s * STEP, STEP)
                gbuf[ns, here, p * half : (p + 1) * half] = (re * ct - im * st).astype(BF16)
                gbuf[ns, here, (slots + p) * half : (slots + p + 1) * half] = (re * st + im * ct).astype(BF16)
        grid = lax.dot_general(gbuf[ns], table[ns], NT, preferred_element_type=F32)
        for s in range(spans):
            size = min(SPAN, quarter - s * SPAN)
            place = first + s * SPAN + iota((total, size), 1)
            keep = place < nlon_s[w if ns == 0 else half - 1 - w]
            out_ref[ns * total : (ns + 1) * total, s * SPAN : s * SPAN + size] = jnp.where(
                keep, grid[s * STEP : s * STEP + total, :size], 0.0
            )
    first_all.wait_send()
    second_all.wait_send()


def shards(spectral, legendre, wave_order, nlon):
    slots, half, width = legendre.shape
    fields = spectral.shape[1]
    waves, levs = lax.axis_size("wave"), lax.axis_size("lev")
    cores = 2
    chips = waves // cores
    side = math.isqrt(chips)
    quarter = (4 * width + 16) // levs
    spans = pl.cdiv(quarter, SPAN)
    hbm = pl.BlockSpec(memory_space=pltpu.HBM)
    dma = pltpu.SemaphoreType.DMA
    order_rows = wave_order.reshape(-1, min(LANES, wave_order.shape[0] // slots))
    grid = pl.pallas_call(
        functools.partial(kernel, chips, cores, levs, quarter),
        out_shape=pltpu.VMEM((2 * fields * levs, quarter), F32),
        in_specs=[hbm] * 5,
        out_specs=pl.BlockSpec(memory_space=pltpu.VMEM),
        scratch_shapes=[
            pltpu.VMEM(spectral.shape, BF16),
            pltpu.SMEM(wave_order.shape, jnp.int32),
            pltpu.SMEM(nlon.shape, jnp.int32),
            pltpu.VMEM(order_rows.shape, jnp.int32),
            pltpu.VMEM((slots, half, width), BF16),
            pltpu.VMEM((slots, 16, width), F32),
            pltpu.VMEM((LANES, half), F32),
            pltpu.VMEM((half, LANES), F32),
            pltpu.VMEM((half, LANES), F32),
            pltpu.VMEM((side, side * cores, LANES), BF16),
            pltpu.VMEM((levs * side, side * cores, LANES), BF16),
            pltpu.VMEM((2, SPAN, 2 * slots * half), BF16),
            pltpu.VMEM((2, slots, 2, 8, half), F32),
            pltpu.VMEM((4 * slots * STEP, half), F32),
            pltpu.VMEM((2, spans * STEP, 2 * slots * half), BF16),
            pltpu.VMEM((16, half), F32),
            dma((4,)),
            dma((slots,)),
            dma,
            dma,
            dma,
            dma,
        ],
        compiler_params=pltpu.CompilerParams(
            collective_id=0, has_side_effects=True, vmem_limit_bytes=64 * 1024 * 1024 - 400000
        ),
    )(spectral, legendre, wave_order, nlon, order_rows)
    return jnp.transpose(grid.reshape(2, fields * levs, quarter), (1, 0, 2))


def solution(mesh):
    placed = (P("wave", "lev", None, None), P("wave", None, None), P(), P())
    return jax.shard_map(
        shards, mesh=mesh, in_specs=placed, out_specs=P(None, "wave", "lev"), check_vma=False
    )
```

time: 36.1 us -> 30.3 us (0.84)
  local copies, waits for them, and re-layouts: 4.92 us -> 0.74 us
  Pallas kernels: 30.9 us -> 29.4 us
    unnamed x8 -> x0, local copies, waits for them, and re-layouts: 4.19 us -> none
    pallas_call x1, Pallas kernels: 30.9 us -> 29.4 us  [shards(): pl.pallas_call(functools.partial(kernel, chips, cores, levs, quarter), ou...]
where the time goes in v2:
time: 30.3 us; the launch traced here: 30.1 us
  Pallas kernels  29.4 us (97%)
  local copies, waits for them, and re-layouts  0.74 us (2%)
    pallas_call x1, Pallas kernels, shards(): pl.pallas_call(functools.partial(kernel, chips, cores, levs, quarter), ou...  29.4 us
    transpose x1, local copies, waits for them, and re-layouts, shards(): return jnp.transpose(grid.reshape(2, fields * levs, quarter), (1, 0, 2))  0.73 us

profile of v2, /device:TPU:1, one launch (start us, length us, event | category | flops | bytes accessed | tf_op | source)
XLA Modules:
  0.0 30.1 jit_solution(8191263806205013919)
XLA Ops:
  0.0 29.4 %shard_map.46 = f32[24,1284]{1,0:T(8,128)S(1)} custom-call(bf16[10,3,2,1280]{3,2,1,0:T(2,128)(2,1)} %spec_hbm.1, bf16[10,128,1280]{2,1,0:T(8,128)(2,1)} %leg_ref.1, s32[1280]{0:T(1024)} %order_hbm.1, s32[128]{0:T(128)} %nlon_hbm.1, s32[10,128]{1,0:T(8,128)} %bitcast.3), custom_call_target="tpu_custom_call" | custom-call | tf_op jit(solution)/shard_map/pallas_call | solution.py:240
  29.4 0.7 %copy.6 = f32[12,2,1284]{2,1,0:T(2,128)} copy(f32[12,2,1284]{2,0,1:T(8,128)S(1)} %bitcast.2) | data formatting | bytes 246528 | tf_op jit(solution)/shard_map/transpose | solution.py:273
  (1 shorter events, 0.0 us)

commit v3 on v2

--- a/solution.py
+++ b/solution.py
@@ -14,6 +14,7 @@
 LANES = 128
 HALF = LANES // 2
 SPAN = 256
+GROUPS = 2
 STEP = 16
 NT = (((1,), (1,)), ((), ()))
 
@@ -60,7 +61,11 @@
             [(spec_hbm, spec_ref), (order_hbm, order_s), (nlon_hbm, nlon_s), (rows_hbm, order_v)]
         )
     ]
-    legs = [pltpu.make_async_copy(leg_ref.at[p], lbuf.at[p], leg_sem.at[p]) for p in range(slots)]
+    cuts = [slots * i // GROUPS for i in range(GROUPS + 1)]
+    legs = [
+        pltpu.make_async_copy(leg_ref.at[a:b], lbuf.at[a:b], leg_sem.at[i])
+        for i, (a, b) in enumerate(zip(cuts, cuts[1:]))
+    ]
 
     side = math.isqrt(chips)
     y, z = chip // side, lax.rem(chip, side)
@@ -104,11 +109,12 @@
             coeffs = jnp.where(live, spec_ref[p, f].astype(F32), 0.0)
             xbuf[p, 2 * f : 2 * f + 2] = coeffs
             xbuf[p, 8 + 2 * f : 8 + 2 * f + 2] = coeffs * parity
-    for p in range(slots):
-        legs[p].wait()
-        sums = lax.dot_general(xbuf[p].astype(BF16), lbuf[p], NT, preferred_element_type=F32)
-        zbuf[n * p : n * p + n] = sums[0:n]
-        zbuf[HALF + n * p : HALF + n * p + n] = sums[8 : 8 + n]
+    for copy, a, b in zip(legs, cuts, cuts[1:]):
+        copy.wait()
+        for p in range(a, b):
+            sums = lax.dot_general(xbuf[p].astype(BF16), lbuf[p], NT, preferred_element_type=F32)
+            zbuf[n * p : n * p + n] = sums[0:n]
+            zbuf[HALF + n * p : HALF + n * p + n] = sums[8 : 8 + n]
 
     total_mates = side * cores
     values = zbuf[...].astype(BF16).astype(F32)
@@ -260,7 +266,7 @@
             pltpu.VMEM((2, spans * STEP, 2 * slots * half), BF16),
             pltpu.VMEM((16, half), F32),
             dma((4,)),
-            dma((slots,)),
+            dma((GROUPS,)),
             dma,
             dma,
             dma,

time: 30.3 us -> 28.3 us (0.934)
  Pallas kernels: 29.4 us -> 27.4 us
    pallas_call x1, Pallas kernels: 29.4 us -> 27.4 us  [shards(): pl.pallas_call(functools.partial(kernel, chips, cores, levs, quarter), ou...]
where the time goes in v3:
time: 28.3 us; the launch traced here: 28.2 us
  Pallas kernels  27.4 us (97%)
  local copies, waits for them, and re-layouts  0.74 us (3%)
    pallas_call x1, Pallas kernels, shards(): pl.pallas_call(functools.partial(kernel, chips, cores, levs, quarter), ou...  27.4 us
    transpose x1, local copies, waits for them, and re-layouts, shards(): return jnp.transpose(grid.reshape(2, fields * levs, quarter), (1, 0, 2))  0.73 us

profile of v3, /device:TPU:1, one launch (start us, length us, event | category | flops | bytes accessed | tf_op | source)
XLA Modules:
  0.0 28.2 jit_solution(13809900936888551865)
XLA Ops:
  0.0 27.4 %shard_map.46 = f32[24,1284]{1,0:T(8,128)S(1)} custom-call(bf16[10,3,2,1280]{3,2,1,0:T(2,128)(2,1)} %spec_hbm.1, bf16[10,128,1280]{2,1,0:T(8,128)(2,1)} %leg_ref.1, s32[1280]{0:T(1024)} %order_hbm.1, s32[128]{0:T(128)} %nlon_hbm.1, s32[10,128]{1,0:T(8,128)} %bitcast.3), custom_call_target="tpu_custom_call" | custom-call | tf_op jit(solution)/shard_map/pallas_call | solution.py:246
  27.4 0.7 %copy.6 = f32[12,2,1284]{2,1,0:T(2,128)} copy(f32[12,2,1284]{2,0,1:T(8,128)S(1)} %bitcast.2) | data formatting | bytes 246528 | tf_op jit(solution)/shard_map/transpose | solution.py:279
  (1 shorter events, 0.0 us)

commit v4 on v3

--- a/solution.py
+++ b/solution.py
@@ -13,7 +13,7 @@
 BF16 = jnp.bfloat16
 LANES = 128
 HALF = LANES // 2
-SPAN = 256
+SPAN = 128
 GROUPS = 2
 STEP = 16
 NT = (((1,), (1,)), ((), ()))
@@ -68,35 +68,32 @@
     ]
 
     side = math.isqrt(chips)
-    y, z = chip // side, lax.rem(chip, side)
-    ys = [lax.rem(y + d, side) for d in range(side)]
-    zs = [lax.rem(z + d, side) for d in range(side)]
+    z, y = chip // side, lax.rem(chip, side)
     cs = [lax.rem(core + d, cores) for d in range(cores)]
     xs = [lax.rem(x + d, levs) for d in range(levs)]
 
     def hops(d, n):
         return min(d, n - d)
 
-    def far_first(n1, n2, weight):
-        pairs = [(d, e) for d in range(n1) for e in range(n2) if d or e]
-        return sorted(pairs, key=lambda d: -hops(d[0], n1) - weight * hops(d[1], n2))
-
-    mates = [(ys[d], cs[e]) for d, e in far_first(side, cores, 0.1)]
-    rest = [(zs[d], xs[e]) for d, e in far_first(side, levs, 1)]
+    def others(mine, n):
+        return [k + (mine <= k).astype(jnp.int32) for k in range(n - 1)]
+
+    far_x = sorted(range(levs), key=lambda d: -hops(d, levs))
+    mates = [(k, c) for k in others(y, side) for c in cs] + [(y, c) for c in cs[1:]]
+    rest = [(k, xs[d]) for k in others(z, side) for d in far_x] + [(z, xs[d]) for d in far_x if d]
 
     def mate_id(there):
-        return ((there[0] * side + z) * cores + there[1], x)
+        return ((z * side + there[0]) * cores + there[1], x)
 
     def rest_id(there):
-        return ((y * side + there[0]) * cores + core, there[1])
+        return ((there[0] * side + y) * cores + core, there[1])
 
     barrier = pltpu.get_barrier_semaphore()
-    for i, there in enumerate([rest_id(r) for r in rest] + [mate_id(r) for r in mates]):
-        if i == side:
-            for copy in inputs + legs:
-                copy.start()
+    for copy in inputs[:2] + legs + inputs[2:]:
+        copy.start()
+    for there in [mate_id(r) for r in mates] + [rest_id(r) for r in rest]:
         pl.semaphore_signal(barrier, inc=1, device_id=there, device_id_type=MESH)
-    for copy in inputs:
+    for copy in inputs[:2]:
         copy.wait()
 
     offset = iota((1, width), 1)
@@ -121,7 +118,7 @@
     north = iota((LANES, half), 0) < HALF
     pair = jnp.concatenate([jnp.where(north, values, 0.0), jnp.where(north, 0.0, values)], 1).astype(BF16)
     r, g = iota((half, 2 * half), 0), iota((half, 2 * half), 1)
-    h = (r // total_mates * side + lax.rem(r, side)) * cores + lax.rem(r // side, cores)
+    h = (r // total_mates + lax.rem(r, side) * side) * cores + lax.rem(r // side, cores)
     route = ((g == h) | ((g == 2 * half - 1 - h) & (g >= half))).astype(F32).astype(BF16)
     send1[...] = lax.dot_general(route, pair, NT, preferred_element_type=F32)
 
@@ -140,9 +137,12 @@
         remote(send1.at[block(there[0] * cores + there[1])], recv1.at[block(own)], (s1_sem, r1_sem), mate_id(there)).start()
     recv1[block(own)] = send1[block(own)]
 
+    for copy in inputs[2:]:
+        copy.wait()
+
     rows_v = order_v.shape[0]
     lane = iota((1, half), 1)
-    device = (lax.rem(lane, total_mates) // cores * side + lane // total_mates) * cores + lax.rem(lane, cores)
+    device = (lax.rem(lane, total_mates) // cores + lane // total_mates * side) * cores + lax.rem(lane, cores)
     high, low = (order_v[...] // 256).astype(F32).astype(BF16), lax.rem(order_v[...], 256).astype(F32).astype(BF16)
     for p in range(slots):
         place = device * slots + p
@@ -177,7 +177,7 @@
 
     first = x * quarter
     spans = pl.cdiv(quarter, SPAN)
-    starts = (first + SPAN * iota((8, half), 0)).astype(F32)
+    starts = (first + SPAN * iota((16, half), 0)).astype(F32)
     for ns in range(2):
         n, inv = counts[ns], inverse[ns]
         for p in range(slots):
@@ -224,7 +224,7 @@
             size = min(SPAN, quarter - s * SPAN)
             place = first + s * SPAN + iota((total, size), 1)
             keep = place < nlon_s[w if ns == 0 else half - 1 - w]
-            out_ref[ns * total : (ns + 1) * total, s * SPAN : s * SPAN + size] = jnp.where(
+            out_ref[:, ns, s * SPAN : s * SPAN + size] = jnp.where(
                 keep, grid[s * STEP : s * STEP + total, :size], 0.0
             )
     first_all.wait_send()
@@ -245,7 +245,7 @@
     order_rows = wave_order.reshape(-1, min(LANES, wave_order.shape[0] // slots))
     grid = pl.pallas_call(
         functools.partial(kernel, chips, cores, levs, quarter),
-        out_shape=pltpu.VMEM((2 * fields * levs, quarter), F32),
+        out_shape=pltpu.VMEM((fields * levs, 2, quarter), F32),
         in_specs=[hbm] * 5,
         out_specs=pl.BlockSpec(memory_space=pltpu.VMEM),
         scratch_shapes=[
@@ -261,7 +261,7 @@
             pltpu.VMEM((side, side * cores, LANES), BF16),
             pltpu.VMEM((levs * side, side * cores, LANES), BF16),
             pltpu.VMEM((2, SPAN, 2 * slots * half), BF16),
-            pltpu.VMEM((2, slots, 2, 8, half), F32),
+            pltpu.VMEM((2, slots, 2, 16, half), F32),
             pltpu.VMEM((4 * slots * STEP, half), F32),
             pltpu.VMEM((2, spans * STEP, 2 * slots * half), BF16),
             pltpu.VMEM((16, half), F32),
@@ -276,7 +276,7 @@
             collective_id=0, has_side_effects=True, vmem_limit_bytes=64 * 1024 * 1024 - 400000
         ),
     )(spectral, legendre, wave_order, nlon, order_rows)
-    return jnp.transpose(grid.reshape(2, fields * levs, quarter), (1, 0, 2))
+    return grid
 
 
 def solution(mesh):

time: 28.3 us -> 26.9 us (0.951)
  Pallas kernels: 27.4 us -> 26.2 us
    pallas_call x1, Pallas kernels: 27.4 us -> 26.2 us  [shards(): pl.pallas_call(functools.partial(kernel, chips, cores, levs, quarter), ou...]
    transpose x1 -> x0, local copies, waits for them, and re-layouts: 0.73 us -> none  [shards(): return jnp.transpose(grid.reshape(2, fields * levs, quarter), (1, 0, 2))]
    unnamed x0 -> x1, local copies, waits for them, and re-layouts: none -> 0.66 us
where the time goes in v4:
time: 26.9 us; the launch traced here: 26.8 us
  Pallas kernels  26.2 us (97%)
  local copies, waits for them, and re-layouts  0.66 us (2%)
    pallas_call x1, Pallas kernels, shards(): pl.pallas_call(functools.partial(kernel, chips, cores, levs, quarter), ou...  26.2 us
    unnamed x1, local copies, waits for them, and re-layouts  0.66 us

profile of v4, /device:TPU:1, one launch (start us, length us, event | category | flops | bytes accessed | tf_op | source)
XLA Modules:
  0.0 26.8 jit_solution(2263931045733264375)
XLA Ops:
  0.0 26.2 %shard_map.46 = f32[12,2,1284]{2,1,0:T(2,128)S(1)} custom-call(bf16[10,3,2,1280]{3,2,1,0:T(2,128)(2,1)} %spec_hbm.1, bf16[10,128,1280]{2,1,0:T(8,128)(2,1)} %leg_ref.1, s32[1280]{0:T(1024)} %order_hbm.1, s32[128]{0:T(128)} %nlon_hbm.1, s32[10,128]{1,0:T(8,128)} %bitcast.1), custom_call_target="tpu_custom_call" | custom-call | tf_op jit(solution)/shard_map/pallas_call | solution.py:246
  26.2 0.7 %copy.6 = f32[12,2,1284]{2,1,0:T(2,128)} copy(f32[12,2,1284]{2,1,0:T(2,128)S(1)} %shard_map.46) | data formatting | bytes 246528

commit v5 on v4

--- a/solution.py
+++ b/solution.py
@@ -79,7 +79,7 @@
         return [k + (mine <= k).astype(jnp.int32) for k in range(n - 1)]
 
     far_x = sorted(range(levs), key=lambda d: -hops(d, levs))
-    mates = [(k, c) for k in others(y, side) for c in cs] + [(y, c) for c in cs[1:]]
+    mates = [(k, c) for k in others(y, side) for c in cs[::-1]] + [(y, c) for c in cs[1:]]
     rest = [(k, xs[d]) for k in others(z, side) for d in far_x] + [(z, xs[d]) for d in far_x if d]
 
     def mate_id(there):

time: 26.9 us -> 26.7 us (level)
  no operation moved by 1% of the time
where the time goes in v5:
time: 26.7 us; the launch traced here: 26.6 us
  Pallas kernels  26 us (97%)
  local copies, waits for them, and re-layouts  0.66 us (2%)
    pallas_call x1, Pallas kernels, shards(): pl.pallas_call(functools.partial(kernel, chips, cores, levs, quarter), ou...  26 us
    unnamed x1, local copies, waits for them, and re-layouts  0.66 us

profile of v5, /device:TPU:1, one launch (start us, length us, event | category | flops | bytes accessed | tf_op | source)
XLA Modules:
  0.0 26.6 jit_solution(15515132091037788144)
XLA Ops:
  0.0 26.0 %shard_map.46 = f32[12,2,1284]{2,1,0:T(2,128)S(1)} custom-call(bf16[10,3,2,1280]{3,2,1,0:T(2,128)(2,1)} %spec_hbm.1, bf16[10,128,1280]{2,1,0:T(8,128)(2,1)} %leg_ref.1, s32[1280]{0:T(1024)} %order_hbm.1, s32[128]{0:T(128)} %nlon_hbm.1, s32[10,128]{1,0:T(8,128)} %bitcast.1), custom_call_target="tpu_custom_call" | custom-call | tf_op jit(solution)/shard_map/pallas_call | solution.py:246
  26.0 0.7 %copy.6 = f32[12,2,1284]{2,1,0:T(2,128)} copy(f32[12,2,1284]{2,1,0:T(2,128)S(1)} %shard_map.46) | data formatting | bytes 246528

commit v6 on v5

--- a/solution.py
+++ b/solution.py
@@ -89,9 +89,10 @@
         return ((there[0] * side + y) * cores + core, there[1])
 
     barrier = pltpu.get_barrier_semaphore()
-    for copy in inputs[:2] + legs + inputs[2:]:
-        copy.start()
-    for there in [mate_id(r) for r in mates] + [rest_id(r) for r in rest]:
+    for i, there in enumerate([mate_id(r) for r in mates] + [rest_id(r) for r in rest]):
+        if i == len(mates):
+            for copy in inputs[:2] + legs + inputs[2:]:
+                copy.start()
         pl.semaphore_signal(barrier, inc=1, device_id=there, device_id_type=MESH)
     for copy in inputs[:2]:
         copy.wait()
@@ -151,6 +152,15 @@
         row = iota((rows_v, half), 0) == place // order_v.shape[1]
         vbuf[p : p + 1] = jnp.sum(jnp.where(row, both, 0.0), 0, keepdims=True)
 
+    most = pl.ds(0, side * (total_mates - 1))
+    first_all = remote(send1.at[most], recv1.at[most], (s1_sem, r1_sem), mate_id(mates[0]))
+    first_all.wait_recv()
+    for i in range(side):
+        send2[i] = recv1[pl.ds(i, total_mates, stride=side)].astype(BF16)
+    for there in rest:
+        remote(send2.at[there[0]], recv2.at[x * side + z], (s2_sem, r2_sem), rest_id(there)).start()
+    recv2[x * side + z] = send2[z]
+
     counts = [nlon_s[w].astype(F32), nlon_s[half - 1 - w].astype(F32)]
     inverse = [1.0 / jnp.full((1, half), n, F32) for n in counts]
     fine = iota((STEP, half), 0).astype(F32)
@@ -165,15 +175,6 @@
                 here = pl.ds(a * STEP, STEP)
                 table[ns, here, p * half : (p + 1) * half] = (c1 * cb - s1 * sb).astype(BF16)
                 table[ns, here, (slots + p) * half : (slots + p + 1) * half] = (-(c1 * sb) - s1 * cb).astype(BF16)
-
-    most = pl.ds(0, side * (total_mates - 1))
-    first_all = remote(send1.at[most], recv1.at[most], (s1_sem, r1_sem), mate_id(mates[0]))
-    first_all.wait_recv()
-    for i in range(side):
-        send2[i] = recv1[pl.ds(i, total_mates, stride=side)].astype(BF16)
-    for there in rest:
-        remote(send2.at[there[0]], recv2.at[x * side + z], (s2_sem, r2_sem), rest_id(there)).start()
-    recv2[x * side + z] = send2[z]
 
     first = x * quarter
     spans = pl.cdiv(quarter, SPAN)

time: 26.7 us -> 26.7 us (level)
  no operation moved by 1% of the time
where the time goes in v6:
time: 26.7 us; the launch traced here: 26.6 us
  Pallas kernels  26 us (97%)
  local copies, waits for them, and re-layouts  0.66 us (2%)
    pallas_call x1, Pallas kernels, shards(): pl.pallas_call(functools.partial(kernel, chips, cores, levs, quarter), ou...  26 us
    unnamed x1, local copies, waits for them, and re-layouts  0.66 us

profile of v6, /device:TPU:1, one launch (start us, length us, event | category | flops | bytes accessed | tf_op | source)
XLA Modules:
  0.0 26.6 jit_solution(14148374556523520627)
XLA Ops:
  0.0 26.0 %shard_map.46 = f32[12,2,1284]{2,1,0:T(2,128)S(1)} custom-call(bf16[10,3,2,1280]{3,2,1,0:T(2,128)(2,1)} %spec_hbm.1, bf16[10,128,1280]{2,1,0:T(8,128)(2,1)} %leg_ref.1, s32[1280]{0:T(1024)} %order_hbm.1, s32[128]{0:T(128)} %nlon_hbm.1, s32[10,128]{1,0:T(8,128)} %bitcast.1), custom_call_target="tpu_custom_call" | custom-call | tf_op jit(solution)/shard_map/pallas_call | solution.py:247
  26.0 0.7 %copy.6 = f32[12,2,1284]{2,1,0:T(2,128)} copy(f32[12,2,1284]{2,1,0:T(2,128)S(1)} %shard_map.46) | data formatting | bytes 246528
